TPU v7x, 256 devices: a whole 4x4x8 slice. The times are simulated.
256 devices in a mesh: ctx: 16 (over y_lo, x, core), tp: 16 (over y_hi, z).
Axes of the slice: x: 4, y: 4 (y_hi: 2, y_lo: 2; y = y_hi * 2 + y_lo), z: 8, core: 2. Of those that a mesh axis runs over, the one named last changes fastest.
Arguments:
- latent: bfloat16 [2048, 5120], P('ctx', 'tp'), may hold values from -2.5 to 2.5
- noise_levels: int32 [3, 16], P(None, 'ctx'), may hold values from 0 to 31, as said below
- mod_table: float32 [32, 2, 5120], replicated, may hold values from -2.5 to 2.5
- w_query: bfloat16 [5120, 4096], P(None, 'tp'), may hold values from -0.078125 to 0.078125
- w_key: bfloat16 [5120, 4096], P(None, 'tp'), may hold values from -0.078125 to 0.078125
- w_value: bfloat16 [5120, 4096], P(None, 'tp'), may hold values from -0.078125 to 0.078125
- w_out: bfloat16 [4096, 5120], P('tp'), may hold values from -0.09375 to 0.09375
- hist_keys: bfloat16 [64, 128, 4096], P('ctx', None, 'tp'), may hold values from -102 to 102
- hist_values: bfloat16 [64, 128, 4096], P('ctx', None, 'tp'), may hold values from -6 to 6
- frame_home: int32 [64], replicated, may hold values from 0 to 63, as said below
- hist_list: int32 [16, 16], P('ctx'), may hold values from 0 to 63, as said below
- list_count: int32 [16], P('ctx'), may hold values from 8 to 16, as said below
Outputs:
- denoised: bfloat16 [2048, 5120], P('ctx', 'tp')
- velocities: bfloat16 [2, 2048, 5120], P(None, 'ctx', 'tp')
Inputs may be any that keep to these rules, and one draw needn't show every extreme that they name: `noise_levels`: for each frame the level falls from each row to the next by 1 to 8. A permutation: frame f lies in slot frame_home[f], held by memory owner frame_home[f] // 4. `hist_list`: row b names, for each of the 16 memory owners, exactly one frame held by that owner; only the first list_count[b] entries are read. `list_count`: some query block reads its whole list.
All inputs are finite; a program needn't handle non-finite values.
Results may differ from a plain program's by a relative error of at most 0.04.
The roundings to bfloat16 on the way count: a program that leaves them out, or rounds other values in their place, can miss the bound.
Values may be sent and summed in bfloat16 or wider, within the bound.
No kernel may reach another device: no remote copies, remote signals or barrier semaphores. Data moves between devices by JAX's collectives and lax.ppermute only.
A program may use at most 128 MiB of HBM per device.

v0:
```python
import math

import jax
import jax.numpy as jnp
from jax import lax
from jax.sharding import PartitionSpec as P

HD = 128


def attend_block(running, query_rows, key_rows, value_rows, key_mask):
    running_max, weight_sum, accumulated = running
    score_scale = 1.0 / math.sqrt(query_rows.shape[2])
    scores = (
        jnp.einsum("qhd,khd->hqk", query_rows, key_rows, preferred_element_type=jnp.float32)
        * score_scale
    )
    scores = jnp.where(key_mask[None], scores, -1e30)
    new_max = jnp.maximum(running_max, jnp.max(scores, axis=-1))
    weights = jnp.where(key_mask[None], jnp.exp(scores - new_max[..., None]), 0.0)
    shrink = jnp.exp(running_max - new_max)
    weight_sum = weight_sum * shrink + jnp.sum(weights, axis=-1)
    accumulated = accumulated * shrink[..., None] + jnp.einsum(
        "hqk,khd->hqd", weights.astype(jnp.bfloat16), value_rows, preferred_element_type=jnp.float32
    )
    return (new_max, weight_sum, accumulated)


def per_device(
    latent,
    noise_levels,
    mod_table,
    w_query,
    w_key,
    w_value,
    w_out,
    hist_keys,
    hist_values,
    frame_home,
    hist_list,
    list_count,
):
    tok_rows = latent.shape[0]
    frames_here = noise_levels.shape[1]
    frame_len = tok_rows // frames_here
    level_count = mod_table.shape[0]
    full_width = mod_table.shape[2]
    head_count = w_query.shape[1] // HD
    ctx_count = lax.axis_size("ctx")
    ctx_id = lax.axis_index("ctx")
    noise_sigma = (noise_levels.astype(jnp.float32) + 1.0) / level_count
    query_frame = (ctx_id * tok_rows + jnp.arange(tok_rows, dtype=jnp.int32)) // frame_len
    slot_per_owner = hist_keys.shape[0]
    past_len = hist_keys.shape[1]
    wanted = frame_home[hist_list[0]]
    owners = wanted // slot_per_owner
    local_slot = wanted % slot_per_owner
    matched = owners[:, None] == jnp.arange(ctx_count, dtype=jnp.int32)[None, :]
    request = jnp.sum(jnp.where(matched, local_slot[:, None], 0), axis=0)
    in_list = jnp.arange(ctx_count, dtype=jnp.int32) < list_count[0]
    valid_owner = jnp.any(matched & in_list[:, None], axis=0)
    asked_slots = lax.all_to_all(request[:, None], "ctx", split_axis=0, concat_axis=0, tiled=True)
    picked = asked_slots[:, 0]
    got_keys, got_values = (
        lax.all_to_all(hist_keys[picked], "ctx", split_axis=0, concat_axis=0, tiled=True),
        lax.all_to_all(hist_values[picked], "ctx", split_axis=0, concat_axis=0, tiled=True),
    )
    past_rows = ctx_count * past_len
    past_keys = got_keys.reshape(past_rows, head_count, HD)
    past_values = got_values.reshape(past_rows, head_count, HD)
    past_mask = jnp.broadcast_to(jnp.repeat(valid_owner, past_len)[None, :], (tok_rows, past_rows))
    latent_now = latent
    velocity_list = []
    for denoise_step in range(2):
        full_latent = lax.all_gather(latent_now, "tp", axis=1, tiled=True)
        onehot = (
            noise_levels[denoise_step][:, None] == jnp.arange(level_count, dtype=jnp.int32)[None, :]
        ).astype(jnp.float32)
        modulation = jnp.einsum("fl,lcd->fcd", onehot, mod_table, precision=lax.Precision.HIGHEST)
        wide_rows = full_latent.astype(jnp.float32).reshape(frames_here, frame_len, full_width)
        meansq = jnp.mean(wide_rows * wide_rows, axis=-1, keepdims=True)
        normed = (
            wide_rows * lax.rsqrt(meansq + 1e-06) * (1.0 + modulation[:, 1][:, None, :])
            + modulation[:, 0][:, None, :]
        )
        normed = normed.astype(jnp.bfloat16).reshape(tok_rows, full_width)
        query_rows = (
            jnp.dot(normed, w_query, preferred_element_type=jnp.float32)
            .astype(jnp.bfloat16)
            .reshape(tok_rows, head_count, HD)
        )
        key_rows = jnp.dot(normed, w_key, preferred_element_type=jnp.float32).astype(jnp.bfloat16)
        value_rows = jnp.dot(normed, w_value, preferred_element_type=jnp.float32).astype(
            jnp.bfloat16
        )
        initial = (
            jnp.full((head_count, tok_rows), -1e30, jnp.float32),
            jnp.zeros((head_count, tok_rows), jnp.float32),
            jnp.zeros((head_count, tok_rows, HD), jnp.float32),
        )
        piece_keys = lax.all_gather(key_rows, "ctx", axis=0, tiled=True)
        piece_values = lax.all_gather(value_rows, "ctx", axis=0, tiled=True)
        piece_len = piece_keys.shape[0]
        key_frame = jnp.arange(piece_len, dtype=jnp.int32) // frame_len
        key_mask = query_frame[:, None] >= key_frame[None, :]
        running = attend_block(
            initial,
            query_rows,
            piece_keys.reshape(piece_len, head_count, HD),
            piece_values.reshape(piece_len, head_count, HD),
            key_mask,
        )
        running_max, weight_sum, accumulated = attend_block(
            running, query_rows, past_keys, past_values, past_mask
        )
        attended = (
            jnp.transpose(accumulated / weight_sum[..., None], (1, 0, 2))
            .reshape(tok_rows, head_count * HD)
            .astype(jnp.bfloat16)
        )
        partial_value = jnp.dot(attended, w_out, preferred_element_type=jnp.float32)
        summed = lax.psum_scatter(partial_value, "tp", scatter_dimension=1, tiled=True)
        velocity = summed.astype(jnp.bfloat16)
        step_size = jnp.repeat(
            noise_sigma[denoise_step + 1] - noise_sigma[denoise_step], frame_len
        )[:, None]
        latent_now = (
            latent_now.astype(jnp.float32) + step_size * velocity.astype(jnp.float32)
        ).astype(jnp.bfloat16)
        velocity_list.append(velocity)
    return (latent_now, jnp.stack(velocity_list))


def solution(mesh):
    return jax.shard_map(
        per_device,
        mesh=mesh,
        in_specs=(
            P("ctx", "tp"),
            P(None, "ctx"),
            P(),
            P(None, "tp"),
            P(None, "tp"),
            P(None, "tp"),
            P("tp", None),
            P("ctx", None, "tp"),
            P("ctx", None, "tp"),
            P(),
            P("ctx", None),
            P("ctx"),
        ),
        out_specs=(P("ctx", "tp"), P(None, "ctx", "tp")),
        check_vma=False,
    )
```

profile of v0, /device:TPU:2, one launch (start us, length us, event | category | flops | bytes accessed | tf_op | source)
XLA Modules:
  0.0 785.4 jit_solution(15803528304609544284)
XLA Ops:
  7.2 0.7 all-gather.7.cloned.1.call-update
  7.9 0.8 fusion.83
  8.7 1.3 gather_fusion
  10.1 0.7 copy.64
  10.8 5.9 all-to-all-start
  16.7 1.4 fusion.97
  18.0 2.8 fusion.22
  20.9 0.4 all-to-all-done
  21.3 0.4 reduce.4
  21.7 1.6 gather_fusion.2
  23.3 5.5 all-to-all-start.2
  28.9 65.2 %all-gather.7.cloned.1.call-done = bf16[128,5120]{0,1:T(8,128)(2,1)} async-done(((bf16[128,320]{0,1:T(8,128)(2,1)}), bf16[128,5120]{0,1:T(8,128)(2,1)}) %all-gather.7.cloned.1.call-update) | async-done | bytes 1310736 | tf_op jit(solution)/shard_map/all_gather | solution.py:75
  94.1 2.2 fusion.4
  96.3 4.1 fusion.7
  100.4 1.1 copy-done.1
  101.5 1.3 convolution_convert_fusion.4
  103.5 1.7 gather_fusion.1
  105.1 4.8 all-to-all-start.1
  110.2 0.2 broadcast_compare_fusion
  110.4 2.2 reshape.354
  112.6 3.7 copy.83
  116.3 9.1 %all-to-all-done.1 = bf16[16,128,256]{2,1,0:T(8,128)(2,1)} async-done(((bf16[16,128,256]{2,1,0:T(8,128)(2,1)}), bf16[16,128,256]{2,1,0:T(8,128)(2,1)}, u32[]{:S(2)}, u32[]{:S(2)}) %all-to-all-start.1) | async-done | bytes 1048608 | tf_op jit(solution)/shard_map/all_to_all | solution.py:65
  125.5 2.2 reshape.353
  127.7 3.7 copy.76
  131.4 3.5 convolution_convert_fusion.3
  135.0 2.9 fusion.34
  137.9 1.8 fusion.100
  139.8 2.0 fusion.99
  141.8 0.9 fusion.12
  142.7 0.4 copy-done.11
  143.1 0.7 copy-done.13
  143.8 0.6 convolution_bitcast_fusion.2
  144.4 32.4 %all-gather.11.cloned.1.call-done = bf16[2048,256]{1,0:T(8,128)(2,1)} async-done(((bf16[128,256]{1,0:T(8,128)(2,1)}), bf16[2048,256]{1,0:T(8,128)(2,1)}) %all-gather.11.cloned.1.call-update) | async-done | bytes 1048592 | tf_op jit(solution)/shard_map/all_gather | solution.py:102
  176.7 2.3 copy.79
  179.0 2.6 fusion.33
  181.6 2.7 fusion.103
  184.3 0.6 copy-done.17
  184.9 0.7 fusion.98
  186.9 210.3 %reduce-scatter.3.cloned.1.call-done = f32[128,320]{0,1:T(8,128)} async-done(((f32[128,5120]{0,1:T(8,128)}), f32[128,320]{0,1:T(8,128)}) %reduce-scatter.3.cloned.1.call-update) | async-done | bytes 163856 | tf_op jit(solution)/shard_map/reduce_scatter | solution.py:122
  397.2 1.6 convert_bitcast_fusion.1
  398.8 0.2 all-gather.15.cloned.1.call-start
  399.0 2.8 fusion.20
  401.9 76.7 %all-gather.13.cloned.1.call-done = bf16[128,5120]{0,1:T(8,128)(2,1)} async-done(((bf16[128,320]{0,1:T(8,128)(2,1)}), bf16[128,5120]{0,1:T(8,128)(2,1)}) %all-gather.13.cloned.1.call-update) | async-done | bytes 1310736 | tf_op jit(solution)/shard_map/all_gather | solution.py:75
  478.6 2.2 fusion.8
  480.7 4.1 fusion.11
  484.8 1.1 copy-done.2
  485.9 1.3 convolution_convert_fusion.1
  487.3 3.5 convolution_convert_fusion
  490.9 2.9 fusion.35
  493.8 1.8 fusion.102
  495.6 23.3 %all-gather.15.cloned.1.call-done = bf16[2048,256]{1,0:T(8,128)(2,1)} async-done(((bf16[128,256]{1,0:T(8,128)(2,1)}), bf16[2048,256]{1,0:T(8,128)(2,1)}) %all-gather.15.cloned.1.call-update) | async-done | bytes 1048592 | tf_op jit(solution)/shard_map/all_gather | solution.py:101
  518.9 2.0 fusion.101
  521.0 0.5 fusion.18
  521.5 0.6 fusion.16
  522.0 0.3 copy-done.12
  522.3 0.6 copy-done.14
  522.9 0.6 convolution_bitcast_fusion
  523.5 32.3 %all-gather.17.cloned.1.call-done = bf16[2048,256]{1,0:T(8,128)(2,1)} async-done(((bf16[128,256]{1,0:T(8,128)(2,1)}), bf16[2048,256]{1,0:T(8,128)(2,1)}) %all-gather.17.cloned.1.call-update) | async-done | bytes 1048592 | tf_op jit(solution)/shard_map/all_gather | solution.py:102
  555.8 2.3 copy.84
  558.1 2.6 fusion.32
  560.7 2.7 fusion.104
  564.7 211.7 %reduce-scatter.5.cloned.1.call-done = f32[128,320]{0,1:T(8,128)} async-done(((f32[128,5120]{0,1:T(8,128)}), f32[128,320]{0,1:T(8,128)}) %reduce-scatter.5.cloned.1.call-update) | async-done | bytes 163856 | tf_op jit(solution)/shard_map/reduce_scatter | solution.py:122
  776.3 1.6 convert_bitcast_fusion
  777.9 0.7 pad_maximum_fusion
  (66 shorter events, 0.9 us)
Async XLA Ops:
  7.2 174.4 %copy-start = (bf16[256,5120]{1,0:T(8,128)(2,1)S(1)}, bf16[256,5120]{1,0:T(8,128)(2,1)}, u32[]{:S(2)}) copy-start(bf16[256,5120]{1,0:T(8,128)(2,1)} %param.18) | copy-start | bytes 7864324
  7.2 14.5 %copy-start.9 = (bf16[4,128,256]{2,1,0:T(8,128)(2,1)S(1)}, bf16[4,128,256]{2,1,0:T(8,128)(2,1)}, u32[]{:S(2)}) copy-start(bf16[4,128,256]{2,1,0:T(8,128)(2,1)} %param.20) | copy-start | bytes 786436
  7.2 86.9 %all-gather.7.cloned.1.call-start = ((), (), s32[]{:S(2)}) async-start(), calls=%async_computation.5 | async-start | bytes 1392640 | tf_op jit(solution)/shard_map/all_gather | solution.py:75
  10.8 10.5 %all-to-all-start = ((s32[16,1,1]{2,1,0:T(1,128)}), s32[16,1,1]{2,1,0:T(1,128)S(1)}, u32[]{:S(2)}, u32[]{:S(2)}) async-start(s32[16,1,1]{2,1,0:T(1,128)} %copy.64), calls=%async_computation | async-start | bytes 16384 | tf_op jit(solution)/shard_map/all_to_all | solution.py:62
  23.3 81.8 %all-to-all-start.2 = ((bf16[16,128,256]{2,1,0:T(8,128)(2,1)}), bf16[16,128,256]{2,1,0:T(8,128)(2,1)}, u32[]{:S(2)}, u32[]{:S(2)}) async-start(bf16[16,128,256]{2,1,0:T(8,128)(2,1)} %gather_fusion.2), calls=%async_computation.2 | async-start | bytes 2097152 | tf_op jit(solution)/shard_map/all_to_all | solution.py:66
  28.8 110.9 %all-gather.9.cloned.1.call-start = ((), (), s32[]{:S(2)}) async-start(), calls=%async_computation.6 | async-start | bytes 1114112 | tf_op jit(solution)/shard_map/all_gather | solution.py:101
  94.1 7.3 copy-start.3
  100.4 1.1 copy-start.1
  101.5 2.0 copy-start.10
  105.1 20.4 %all-to-all-start.1 = ((bf16[16,128,256]{2,1,0:T(8,128)(2,1)}), bf16[16,128,256]{2,1,0:T(8,128)(2,1)}, u32[]{:S(2)}, u32[]{:S(2)}) async-start(bf16[16,128,256]{2,1,0:T(8,128)(2,1)} %gather_fusion.1), calls=%async_computation.1 | async-start | bytes 2097152 | tf_op jit(solution)/shard_map/all_to_all | solution.py:65
  110.0 66.7 %all-gather.11.cloned.1.call-start = ((), (), s32[]{:S(2)}) async-start(), calls=%async_computation.7 | async-start | bytes 1114112 | tf_op jit(solution)/shard_map/all_gather | solution.py:102
  134.9 262.3 %reduce-scatter.3.cloned.1.call-start = ((), (), s32[]{:S(2)}) async-start(), calls=%async_computation.8 | async-start | bytes 2785280 | tf_op jit(solution)/shard_map/reduce_scatter | solution.py:122
  135.0 2.9 copy-start.5
  139.8 2.0 copy-start.7
  141.8 1.3 copy-start.11
  141.8 2.0 copy-start.13
  184.3 0.7 copy-start.17
  184.3 212.9 %copy-start.16 = (bf16[128,320]{0,1:T(8,128)(2,1)S(1)}, bf16[128,320]{0,1:T(8,128)(2,1)}, u32[]{:S(2)}) copy-start(bf16[128,320]{0,1:T(8,128)(2,1)} %param.12) | copy-start | bytes 245764
  184.3 294.3 %all-gather.13.cloned.1.call-start = ((), (), s32[]{:S(2)}) async-start(), calls=%async_computation.9 | async-start | bytes 1392640 | tf_op jit(solution)/shard_map/all_gather | solution.py:75
  398.8 120.1 %all-gather.15.cloned.1.call-start = ((), (), s32[]{:S(2)}) async-start(), calls=%async_computation.10 | async-start | bytes 1114112 | tf_op jit(solution)/shard_map/all_gather | solution.py:101
  478.6 7.4 copy-start.4
  484.8 1.1 copy-start.2
  487.3 68.6 %all-gather.17.cloned.1.call-start = ((), (), s32[]{:S(2)}) async-start(), calls=%async_computation.11 | async-start | bytes 1114112 | tf_op jit(solution)/shard_map/all_gather | solution.py:102
  490.8 285.5 %reduce-scatter.5.cloned.1.call-start = ((), (), s32[]{:S(2)}) async-start(), calls=%async_computation.12 | async-start | bytes 2785280 | tf_op jit(solution)/shard_map/reduce_scatter | solution.py:122
  490.8 2.9 copy-start.6
  518.9 2.1 copy-start.8
  520.9 1.4 copy-start.12
  521.0 2.0 copy-start.14
  563.4 213.0 %copy-start.15 = (bf16[128,320]{0,1:T(8,128)(2,1)S(1)}, bf16[128,320]{0,1:T(8,128)(2,1)}, u32[]{:S(2)}) copy-start(bf16[128,320]{0,1:T(8,128)(2,1)} %get-tuple-element.7) | copy-start | bytes 245764
Sparse Core Ops, SparseCore 0:
  10.6 83.4 all-gather.6
  102.9 36.0 all-gather.8
  141.4 35.2 all-gather.10
  184.4 212.7 reduce-scatter.2
  400.2 78.3 all-gather.12
  487.4 31.4 all-gather.14
  520.8 35.0 all-gather.16
  563.5 212.7 reduce-scatter.4
where the time goes:
time: 786 us; the launch traced here: 785 us
  waiting for transfers between devices  662 us (84%)
  matrix products  40.4 us (5%)
  local copies, waits for them, and re-layouts  28.5 us (4%)
  other arithmetic  20 us (3%)
  between operations  17.7 us (2%)
  starting transfers between devices  16.8 us (2%)
    reduce_scatter x2, waiting for transfers between devices, per_device(): lax.psum_scatter(partial_value, 'tp', scatter_dimension=1, tiled=True)  422 us
    all_gather x2, waiting for transfers between devices, per_device(): full_latent = lax.all_gather(latent_now, 'tp', axis=1, tiled=True)  142 us
    all_gather x2, waiting for transfers between devices, per_device(): piece_values = lax.all_gather(value_rows, 'ctx', axis=0, tiled=True)  64.7 us
    all_gather x2, waiting for transfers between devices, per_device(): piece_keys = lax.all_gather(key_rows, 'ctx', axis=0, tiled=True)  23.3 us
  transfers between devices with their start and end apart: 11, of which 9 were waited for; matrix products, arithmetic and copies ran while one was open for 7% of the time, Pallas kernels for 0%

commit v1 on v0

v1 whole, which is shorter than its diff:
```python
import math

import jax
import jax.numpy as jnp
from jax import lax
from jax.sharding import Mesh, PartitionSpec as P

HD = 128
CTX = ("yl", "x", "core")
CHIPS = ("yl", "x")
TP = ("yh", "z")


def per_device(
    latent,
    noise_levels,
    mod_table,
    w_query,
    w_key,
    w_value,
    w_out,
    hist_keys,
    hist_values,
    frame_home,
    hist_list,
    list_count,
):
    tok, width = latent.shape
    level_count, _, full = mod_table.shape
    heads = w_query.shape[1] // HD
    hw = heads * HD
    n_ctx = lax.axis_size(CTX)
    n_chip = lax.axis_size(CHIPS)
    n_tp = lax.axis_size(TP)
    n_z = lax.axis_size("z")
    core = lax.axis_index("core")
    chip = lax.axis_index(CHIPS)
    tp_id = lax.axis_index(TP)
    rows = tok // n_tp
    f32, bf16 = jnp.float32, jnp.bfloat16
    scale = 1.0 / math.sqrt(HD)
    swap = [(0, 1), (1, 0)]

    sigma = (noise_levels[:, 0].astype(f32) + 1.0) / level_count
    steps = sigma[1:] - sigma[:-1]

    slot_per_owner, past_len, _ = hist_keys.shape
    wanted = frame_home[hist_list[0]]
    matched = (wanted // slot_per_owner)[:, None] == jnp.arange(n_ctx, dtype=jnp.int32)[None, :]
    request = jnp.sum(jnp.where(matched, (wanted % slot_per_owner)[:, None], 0), axis=0)
    in_list = jnp.arange(n_ctx, dtype=jnp.int32) < list_count[0]
    valid_owner = jnp.any(matched & in_list[:, None], axis=0)
    picked = lax.all_to_all(request[:, None], CTX, split_axis=0, concat_axis=0, tiled=True)[:, 0]
    hist = jnp.concatenate([hist_keys, hist_values], axis=2)
    past = lax.all_to_all(hist[picked], CTX, split_axis=0, concat_axis=0, tiled=True)

    own = latent.T
    other = lax.ppermute(own, "yh", swap)
    is_hi = lax.axis_index("yh") == 1
    pair = jnp.stack([jnp.where(is_hi, other, own), jnp.where(is_hi, own, other)])
    gathered = lax.all_gather(pair, "z", axis=0)
    full_t = jnp.transpose(gathered, (1, 0, 2, 3)).reshape(full, tok)
    full_rows = full_t.T

    def norm(x, step):
        mod = mod_table[noise_levels[step, 0]]
        wide = x.astype(f32)
        meansq = jnp.mean(wide * wide, axis=-1, keepdims=True)
        out = wide * lax.rsqrt(meansq + 1e-06) * (1.0 + mod[1][None]) + mod[0][None]
        return out.astype(bf16)

    own_rows = lax.dynamic_slice_in_dim(full_rows, tp_id * rows, rows, 0)
    normed = norm(full_rows, 0)

    chips = jnp.arange(n_chip, dtype=jnp.int32)
    seen_own = chips <= chip
    seen_other = (chips < chip) | ((chips == chip) & (core == 1))
    live = jnp.concatenate([seen_own, seen_other, valid_owner])
    live = jnp.repeat(live, tok)[None, None, :]

    def attend(normed):
        k = jnp.dot(normed, w_key, preferred_element_type=f32).astype(bf16)
        v = jnp.dot(normed, w_value, preferred_element_type=f32).astype(bf16)
        kv = jnp.concatenate([k, v], axis=1)
        near = lax.all_to_all(
            jnp.broadcast_to(kv[None], (n_chip, tok, 2 * hw)), CHIPS, split_axis=0, concat_axis=0, tiled=True
        )
        far = lax.ppermute(near, "core", swap)
        q = jnp.dot(normed, w_query, preferred_element_type=f32).astype(bf16).reshape(tok, heads, HD)
        every = jnp.concatenate([near, far, past], axis=0).reshape(-1, 2 * hw)
        keys = every[:, :hw].reshape(-1, heads, HD)
        values = every[:, hw:].reshape(-1, heads, HD)
        scores = jnp.einsum("qhd,khd->hqk", q, keys, preferred_element_type=f32) * scale
        scores = jnp.where(live, scores, -1e30)
        top = jnp.max(scores, axis=-1, keepdims=True)
        weights = jnp.where(live, jnp.exp(scores - top), 0.0)
        total = jnp.sum(weights, axis=-1)
        acc = jnp.einsum("hqk,khd->hqd", weights.astype(bf16), values, preferred_element_type=f32)
        out = jnp.transpose(acc / total[..., None], (1, 0, 2)).reshape(tok, hw).astype(bf16)
        return jnp.dot(out, w_out, preferred_element_type=f32).astype(bf16)

    part = attend(normed).reshape(n_tp, rows, full)
    got = lax.all_to_all(part, TP, split_axis=0, concat_axis=0, tiled=True)
    v0_rows = jnp.sum(got.astype(f32), axis=0).astype(bf16)
    x1_rows = (own_rows.astype(f32) + steps[0] * v0_rows.astype(f32)).astype(bf16)
    normed_rows = norm(x1_rows, 1)
    pad = -width % 128
    v0_send = jnp.pad(jnp.transpose(v0_rows.reshape(rows, n_tp, width), (1, 0, 2)), ((0, 0), (0, 0), (0, pad)))
    send = jnp.concatenate([jnp.broadcast_to(normed_rows[None], (n_tp, rows, full)), v0_send], axis=2)
    got = lax.all_to_all(send, TP, split_axis=0, concat_axis=0, tiled=True)
    normed = got[:, :, :full].reshape(tok, full)
    v0 = got[:, :, full : full + width].reshape(tok, width)
    x1 = (latent.astype(f32) + steps[0] * v0.astype(f32)).astype(bf16)

    part = attend(normed)
    part = jnp.transpose(part.reshape(tok, n_tp, width), (1, 2, 0))
    got = lax.all_to_all(part, TP, split_axis=0, concat_axis=0, tiled=True)
    v1 = jnp.sum(got.astype(f32), axis=0).astype(bf16).T
    x2 = (x1.astype(f32) + steps[1] * v1.astype(f32)).astype(bf16)
    return x2, jnp.stack([v0, v1])


def solution(mesh):
    fine = Mesh(mesh.devices.reshape(2, 4, 2, 2, 8), ("yl", "x", "core", "yh", "z"))
    return jax.shard_map(
        per_device,
        mesh=fine,
        in_specs=(
            P(CTX, TP),
            P(None, CTX),
            P(),
            P(None, TP),
            P(None, TP),
            P(None, TP),
            P(TP, None),
            P(CTX, None, TP),
            P(CTX, None, TP),
            P(),
            P(CTX, None),
            P(CTX),
        ),
        out_specs=(P(CTX, TP), P(None, CTX, TP)),
        check_vma=False,
    )
```

time: 786 us -> 324 us (0.41)
  waiting for transfers between devices: 662 us -> 125 us
  blocking collectives: 0 us -> 57.2 us
  starting transfers between devices: 16.8 us -> 34.5 us
  matrix products: 40.4 us -> 24.2 us
  local copies, waits for them, and re-layouts: 28.5 us -> 41 us
    reduce_scatter x2 -> x0, waiting for transfers between devices: 422 us -> none  [per_device(): lax.psum_scatter(partial_value, 'tp', scatter_dimension=1, tiled=True)]
    all_gather x6 -> x1, waiting for transfers between devices: 230 us -> 27.9 us  [per_device(): gathered = lax.all_gather(pair, 'z', axis=0)]
    all_to_all x3 -> x5, waiting for transfers between devices: 9.53 us -> 92.5 us  [the longest x2 60.6 us: per_device(): got = lax.all_to_all(part, TP, split_axis=0, concat_axis=0, tiled=True)]
    all_to_all x0 -> x2, blocking collectives: none -> 57.2 us  [the longest x1 40.8 us: per_device(): got = lax.all_to_all(send, TP, split_axis=0, concat_axis=0, tiled=True)]
    dot_general x18 -> x10, matrix products: 40.4 us -> 14.9 us  [the longest x2 5.85 us: attend(): jnp.einsum('hqk,khd->hqd', weights.astype(bf16), values, preferred_elemen...]
    unnamed x36 -> x30, local copies, waits for them, and re-layouts: 4.74 us -> 21.3 us
    reshape x6 -> x1, local copies, waits for them, and re-layouts: 16.4 us -> 0.14 us  [per_device(): v0_rows.reshape(rows, n_tp, width)]
    all_to_all x3 -> x5, starting transfers between devices: 16.3 us -> 31 us  [the longest x2 14.1 us: per_device(): got = lax.all_to_all(part, TP, split_axis=0, concat_axis=0, tiled=True)]
  transfers between devices with their start and end apart: 11 -> 9, of which waited for: 9 -> 7; matrix products, arithmetic and copies ran while one was open for 7% -> 8% of each run, Pallas kernels for 0% -> 0%
where the time goes in v1:
time: 324 us; the launch traced here: 322 us
  waiting for transfers between devices  125 us (39%)
  blocking collectives  57.2 us (18%)
  local copies, waits for them, and re-layouts  41 us (13%)
  starting transfers between devices  34.5 us (11%)
  matrix products  24.2 us (7%)
  other arithmetic  20.9 us (6%)
  between operations  18.7 us (6%)
    all_to_all x2, waiting for transfers between devices, per_device(): got = lax.all_to_all(part, TP, split_axis=0, concat_axis=0, tiled=True)  60.6 us
    all_to_all x1, blocking collectives, per_device(): got = lax.all_to_all(send, TP, split_axis=0, concat_axis=0, tiled=True)  40.8 us
    all_gather x1, waiting for transfers between devices, per_device(): gathered = lax.all_gather(pair, 'z', axis=0)  27.9 us
    all_to_all x1, waiting for transfers between devices, per_device(): lax.all_to_all(hist[picked], CTX, split_axis=0, concat_axis=0, tiled=True)  24.8 us
    unnamed x30, local copies, waits for them, and re-layouts  21.3 us
    all_to_all x1, blocking collectives, attend(): lax.all_to_all(jnp.broadcast_to(kv[None], (n_chip, tok, 2 * hw)), CHIPS,...  16.4 us
    all_to_all x2, starting transfers between devices, per_device(): got = lax.all_to_all(part, TP, split_axis=0, concat_axis=0, tiled=True)  14.1 us
    sub x2, matrix products, attend(): weights = jnp.where(live, jnp.exp(scores - top), 0.0)  9.29 us
  transfers between devices with their start and end apart: 9, of which 7 were waited for; matrix products, arithmetic and copies ran while one was open for 8% of the time, Pallas kernels for 0%

profile of v1, /device:TPU:2, one launch (start us, length us, event | category | flops | bytes accessed | tf_op | source)
XLA Modules:
  0.0 322.0 jit_solution(13911360126541489539)
XLA Ops:
  7.2 3.3 %collective-permute-start = (bf16[320,128]{1,0:T(8,128)(2,1)}, bf16[320,128]{1,0:T(8,128)(2,1)S(1)}, u32[]{:S(2)}, u32[]{:S(2)}) collective-permute-start(bf16[320,128]{1,0:T(8,128)(2,1)} %bitcast.137), channel_id=1, source_target_pairs={{0,8},{8,0},{1,9},{9,1},{2,10},{10,2},{3,11},{11,3},{4,12},{12,4},... | collective-permute-start | bytes 245768 | tf_op jit(solution)/shard_map/ppermute | solution.py:58
  10.5 3.0 collective-permute-done
  13.5 0.9 select_bitcast_fusion.1
  14.4 0.7 pad_maximum_fusion.3
  15.1 0.7 fusion.66
  15.7 1.3 gather_fusion
  17.2 0.7 copy.73
  17.9 5.9 %all-to-all-start.1 = ((s32[16,1,1]{2,1,0:T(1,128)}), s32[16,1,1]{2,1,0:T(1,128)S(1)}, u32[]{:S(2)}, u32[]{:S(2)}) async-start(s32[16,1,1]{2,1,0:T(1,128)} %copy.73), calls=%async_computation.1 | async-start | bytes 16384 | tf_op jit(solution)/shard_map/all_to_all | solution.py:53
  23.7 1.3 fusion.75
  28.7 0.9 dynamic-slice_add_fusion
  29.6 27.9 %all-gather.3.cloned.1.call-done = bf16[16,320,128]{2,1,0:T(8,128)(2,1)} async-done(((bf16[2,320,128]{2,1,0:T(8,128)(2,1)}), bf16[16,320,128]{2,1,0:T(8,128)(2,1)}) %all-gather.3.cloned.1.call-update) | async-done | bytes 1310736 | tf_op jit(solution)/shard_map/all_gather | solution.py:61
  57.5 1.4 copy.71
  59.0 0.8 fusion.12
  59.8 2.8 fusion.15
  62.6 0.7 convolution_convert_fusion.6
  63.4 1.5 copy-done.5
  64.8 0.7 convolution_convert_fusion.5
  65.6 1.1 broadcast_in_dim.77
  66.7 5.7 %all-to-all-start = ((bf16[8,128,512]{2,1,0:T(8,128)(2,1)}), bf16[8,128,512]{2,1,0:T(8,128)(2,1)}, u32[]{:S(2)}, u32[]{:S(2)}) async-start(bf16[8,128,512]{2,1,0:T(8,128)(2,1)} %broadcast_in_dim.77), calls=%async_computation | async-start | bytes 2097152 | tf_op jit(solution)/shard_map/all_to_all | solution.py:85
  72.4 1.0 pad_maximum_fusion.2
  73.4 0.4 reduce.3
  73.8 2.0 gather_fusion.1
  75.8 7.1 %all-to-all-done = bf16[8,128,512]{2,1,0:T(8,128)(2,1)} async-done(((bf16[8,128,512]{2,1,0:T(8,128)(2,1)}), bf16[8,128,512]{2,1,0:T(8,128)(2,1)}, u32[]{:S(2)}, u32[]{:S(2)}) %all-to-all-start) | async-done | bytes 1048608 | tf_op jit(solution)/shard_map/all_to_all | solution.py:85
  82.9 5.3 %all-to-all-start.2 = ((bf16[16,128,512]{2,1,0:T(8,128)(2,1)}), bf16[16,128,512]{2,1,0:T(8,128)(2,1)}, u32[]{:S(2)}, u32[]{:S(2)}) async-start(bf16[16,128,512]{2,1,0:T(8,128)(2,1)} %gather_fusion.1), calls=%async_computation.2 | async-start | bytes 4194304 | tf_op jit(solution)/shard_map/all_to_all | solution.py:55
  88.2 0.1 collective-permute-start.1
  89.3 2.8 fusion.39
  92.1 24.8 %all-to-all-done.2 = bf16[16,128,512]{2,1,0:T(8,128)(2,1)} async-done(((bf16[16,128,512]{2,1,0:T(8,128)(2,1)}), bf16[16,128,512]{2,1,0:T(8,128)(2,1)}, u32[]{:S(2)}, u32[]{:S(2)}) %all-to-all-start.2) | async-done | bytes 2097184 | tf_op jit(solution)/shard_map/all_to_all | solution.py:55
  116.9 2.4 pad_maximum_fusion.1
  119.3 2.3 fusion.73
  121.6 4.1 %copy.89 = bf16[4096,256]{0,1:T(8,128)(2,1)} copy(bf16[4096,256]{1,0:T(8,128)(2,1)} %get-tuple-element.8) | data formatting | bytes 4194304
  125.7 4.1 %copy.90 = bf16[4096,256]{0,1:T(8,128)(2,1)} copy(bf16[4096,256]{1,0:T(8,128)(2,1)} %get-tuple-element.9) | data formatting | bytes 4194304
  129.8 4.7 %fusion.76 = (f32[2,128]{1,0:T(2,128)S(1)}, bf16[2,128,4096]{2,1,0:T(8,128)(2,1)}) fusion(bf16[4096,2,128]{0,2,1:T(8,128)(2,1)} %bitcast.132, pred[4096]{0:T(1024)(128)(4,1)S(1)} %broadcast_bitcast_fusion, bf16[16,2,8,128]{3,2,1,0:T(8,128)(2,1)S(1)} %fusion.39), kind=kOutput, calls=%fused_computation.113 | convolution fusion | flops 274731008 | bytes 4264960 | tf_op jit(solution)/shard_map/sub | solution.py:96
  134.5 2.9 fusion.36
  137.4 1.6 fusion.4
  139.0 7.0 %all-to-all-start.3 = ((bf16[16,8,5120]{2,1,0:T(8,128)(2,1)}), bf16[16,8,5120]{2,1,0:T(8,128)(2,1)}, u32[]{:S(2)}, u32[]{:S(2)}) async-start(bf16[16,8,5120]{2,1,0:T(8,128)(2,1)} %fusion.4), calls=%async_computation.3 | async-start | bytes 2621440 | tf_op jit(solution)/shard_map/all_to_all | solution.py:103
  146.2 0.6 fusion.74
  146.7 2.9 constant_dynamic-slice_fusion.2
  149.6 1.7 copy.88
  151.3 28.9 %all-to-all-done.3 = bf16[16,8,5120]{2,1,0:T(8,128)(2,1)} async-done(((bf16[16,8,5120]{2,1,0:T(8,128)(2,1)}), bf16[16,8,5120]{2,1,0:T(8,128)(2,1)}, u32[]{:S(2)}, u32[]{:S(2)}) %all-to-all-start.3) | async-done | bytes 1310752 | tf_op jit(solution)/shard_map/all_to_all | solution.py:103
  180.1 1.5 reduce_sum.72
  181.8 0.8 fusion.41
  182.6 0.7 fusion.44
  183.6 40.8 %all_to_all.42 = bf16[16,8,5504]{2,1,0:T(8,128)(2,1)S(1)} all-to-all(bf16[16,8,5504]{2,1,0:T(8,128)(2,1)S(1)} %fusion.20), channel_id=1, replica_groups=mesh['yl'=2,'x'=4,'core'=2,'yh'=2,'z'=8] {'yh','z'}, dimensions={0} | all-to-all | bytes 2818048 | tf_op jit(solution)/shard_map/all_to_all | solution.py:110
  224.4 0.5 convolution_convert_fusion.3
  225.0 1.7 copy-done.6
  226.7 0.5 convolution_convert_fusion.2
  227.4 16.4 %all_to_all.43 = bf16[8,128,512]{2,1,0:T(8,128)(2,1)S(1)} all-to-all(bf16[8,128,512]{2,1,0:T(8,128)(2,1)S(1)} %broadcast_in_dim.83), channel_id=1, replica_groups=mesh['yl'=2,'x'=4,'core'=2,'yh'=2,'z'=8] {'yl','x'}, dimensions={0} | all-to-all | bytes 2097152 | tf_op jit(solution)/shard_map/all_to_all | solution.py:85
  243.7 0.5 fusion.40
  244.3 2.1 collective-permute-done.2
  246.4 1.8 pad_maximum_fusion
  248.1 2.2 fusion.72
  250.4 4.1 %copy.91 = bf16[4096,256]{0,1:T(8,128)(2,1)} copy(bf16[4096,256]{1,0:T(8,128)(2,1)} %get-tuple-element.6) | data formatting | bytes 4194304
  254.5 4.1 %copy.92 = bf16[4096,256]{0,1:T(8,128)(2,1)} copy(bf16[4096,256]{1,0:T(8,128)(2,1)} %get-tuple-element.7) | data formatting | bytes 4194304
  258.5 4.6 %fusion.79 = (f32[2,128]{1,0:T(2,128)S(1)}, bf16[2,128,4096]{2,1,0:T(8,128)(2,1)}) fusion(bf16[4096,2,128]{0,2,1:T(8,128)(2,1)} %bitcast.130, pred[4096]{0:T(1024)(128)(4,1)S(1)} %broadcast_bitcast_fusion, bf16[16,2,8,128]{3,2,1,0:T(8,128)(2,1)S(1)} %fusion.40), kind=kOutput, calls=%fused_computation.114 | convolution fusion | flops 274731008 | bytes 4264960 | tf_op jit(solution)/shard_map/sub | solution.py:96
  263.2 2.9 fusion.33
  266.1 1.6 convolution_convert_fusion
  267.7 2.4 copy.82
  270.1 7.1 %all-to-all-start.6 = ((bf16[16,320,128]{2,1,0:T(8,128)(2,1)}), bf16[16,320,128]{2,1,0:T(8,128)(2,1)}, u32[]{:S(2)}, u32[]{:S(2)}) async-start(bf16[16,320,128]{2,1,0:T(8,128)(2,1)} %bitcast.129), calls=%async_computation.6 | async-start | bytes 2621440 | tf_op jit(solution)/shard_map/all_to_all | solution.py:117
  277.2 1.6 multiply_bitcast_fusion
  278.9 0.9 slice_bitcast_fusion.4
  279.9 31.7 %all-to-all-done.6 = bf16[16,320,128]{2,1,0:T(8,128)(2,1)} async-done(((bf16[16,320,128]{2,1,0:T(8,128)(2,1)}), bf16[16,320,128]{2,1,0:T(8,128)(2,1)}, u32[]{:S(2)}, u32[]{:S(2)}) %all-to-all-start.6) | async-done | bytes 1310752 | tf_op jit(solution)/shard_map/all_to_all | solution.py:117
  311.6 1.5 reduce_sum.75
  313.2 1.3 add_convert_fusion
  314.5 0.7 pad_maximum_fusion.4
  (50 shorter events, 1.3 us)
Async XLA Ops:
  7.2 130.2 %copy-start = (bf16[256,5120]{1,0:T(8,128)(2,1)S(1)}, bf16[256,5120]{1,0:T(8,128)(2,1)}, u32[]{:S(2)}) copy-start(bf16[256,5120]{1,0:T(8,128)(2,1)} %param.18) | copy-start | bytes 7864324
  7.2 50.4 %all-gather.3.cloned.1.call-start = ((), (), s32[]{:S(2)}) async-start(), calls=%async_computation.7 | async-start | bytes 1474560 | tf_op jit(solution)/shard_map/all_gather | solution.py:61
  7.2 6.2 %collective-permute-start = (bf16[320,128]{1,0:T(8,128)(2,1)}, bf16[320,128]{1,0:T(8,128)(2,1)S(1)}, u32[]{:S(2)}, u32[]{:S(2)}) collective-permute-start(bf16[320,128]{1,0:T(8,128)(2,1)} %bitcast.137), channel_id=1, source_target_pairs={{0,8},{8,0},{1,9},{9,1},{2,10},{10,2},{3,11},{11,3},{4,12},{12,4},... | collective-permute-start | bytes 245768 | tf_op jit(solution)/shard_map/ppermute | solution.py:58
  17.9 47.7 %all-to-all-start.1 = ((s32[16,1,1]{2,1,0:T(1,128)}), s32[16,1,1]{2,1,0:T(1,128)S(1)}, u32[]{:S(2)}, u32[]{:S(2)}) async-start(s32[16,1,1]{2,1,0:T(1,128)} %copy.73), calls=%async_computation.1 | async-start | bytes 16384 | tf_op jit(solution)/shard_map/all_to_all | solution.py:53
  58.9 4.4 %copy-start.1 = (bf16[2,8,320,128]{3,2,1,0:T(8,128)(2,1)}, bf16[2,8,320,128]{3,2,1,0:T(8,128)(2,1)S(1)}, u32[]{:S(2)}) copy-start(bf16[2,8,320,128]{3,2,1,0:T(8,128)(2,1)S(1)} %copy.71) | copy-start | bytes 3932164
  59.0 3.6 %copy-start.3 = (bf16[5120,256]{1,0:T(8,128)(2,1)S(1)}, bf16[5120,256]{1,0:T(8,128)(2,1)}, u32[]{:S(2)}) copy-start(bf16[5120,256]{1,0:T(8,128)(2,1)} %param.16) | copy-start | bytes 7864324
  62.6 2.9 copy-start.2
  62.6 2.2 copy-start.5
  65.5 6.9 %copy-start.10 = (bf16[4,128,256]{2,1,0:T(8,128)(2,1)S(1)}, bf16[4,128,256]{2,1,0:T(8,128)(2,1)}, u32[]{:S(2)}) copy-start(bf16[4,128,256]{2,1,0:T(8,128)(2,1)} %param.20) | copy-start | bytes 786436
  66.7 16.2 %all-to-all-start = ((bf16[8,128,512]{2,1,0:T(8,128)(2,1)}), bf16[8,128,512]{2,1,0:T(8,128)(2,1)}, u32[]{:S(2)}, u32[]{:S(2)}) async-start(bf16[8,128,512]{2,1,0:T(8,128)(2,1)} %broadcast_in_dim.77), calls=%async_computation | async-start | bytes 2097152 | tf_op jit(solution)/shard_map/all_to_all | solution.py:85
  82.9 34.0 %all-to-all-start.2 = ((bf16[16,128,512]{2,1,0:T(8,128)(2,1)}), bf16[16,128,512]{2,1,0:T(8,128)(2,1)}, u32[]{:S(2)}, u32[]{:S(2)}) async-start(bf16[16,128,512]{2,1,0:T(8,128)(2,1)} %gather_fusion.1), calls=%async_computation.2 | async-start | bytes 4194304 | tf_op jit(solution)/shard_map/all_to_all | solution.py:55
  88.2 28.7 %collective-permute-start.1 = (bf16[8,128,512]{2,1,0:T(8,128)(2,1)}, bf16[8,128,512]{2,1,0:T(8,128)(2,1)}, u32[]{:S(2)}, u32[]{:S(2)}) collective-permute-start(bf16[8,128,512]{2,1,0:T(8,128)(2,1)} %all-to-all-done), channel_id=1, source_target_pairs={{0,16},{16,0},{1,17},{17,1},{2,18},{18,2},{3,19},{19,3},{4,20},{20... | collective-permute-start | bytes 3145736 | tf_op jit(solution)/shard_map/ppermute | solution.py:88
  139.0 7.1 %copy-start.11 = (s32[3,1]{0,1:T(1,128)S(1)}, s32[3,1]{0,1:T(1,128)}, u32[]{:S(2)}) copy-start(s32[3,1]{0,1:T(1,128)} %param.13) | copy-start | bytes 40
  139.0 41.1 %all-to-all-start.3 = ((bf16[16,8,5120]{2,1,0:T(8,128)(2,1)}), bf16[16,8,5120]{2,1,0:T(8,128)(2,1)}, u32[]{:S(2)}, u32[]{:S(2)}) async-start(bf16[16,8,5120]{2,1,0:T(8,128)(2,1)} %fusion.4), calls=%async_computation.3 | async-start | bytes 2621440 | tf_op jit(solution)/shard_map/all_to_all | solution.py:103
  183.6 40.8 %copy-start.4 = (bf16[5120,256]{1,0:T(8,128)(2,1)S(1)}, bf16[5120,256]{1,0:T(8,128)(2,1)}, u32[]{:S(2)}) copy-start(bf16[5120,256]{1,0:T(8,128)(2,1)} %param.16) | copy-start | bytes 7864324
  224.4 19.3 %copy-start.8 = (bf16[16,8,5504]{2,1,0:T(8,128)(2,1)}, bf16[16,8,5504]{2,1,0:T(8,128)(2,1)S(1)}, u32[]{:S(2)}) copy-start(bf16[16,8,5504]{2,1,0:T(8,128)(2,1)S(1)} %all_to_all.42) | copy-start | bytes 4227076
  224.4 2.3 copy-start.6
  227.2 16.5 %copy-start.7 = (bf16[5120,256]{1,0:T(8,128)(2,1)S(1)}, bf16[5120,256]{1,0:T(8,128)(2,1)}, u32[]{:S(2)}) copy-start(bf16[5120,256]{1,0:T(8,128)(2,1)} %param.15) | copy-start | bytes 7864324
  243.7 2.7 collective-permute-start.2
  270.1 43.0 %copy-start.9 = (bf16[128,320]{0,1:T(8,128)(2,1)S(1)}, bf16[128,320]{0,1:T(8,128)(2,1)}, u32[]{:S(2)}) copy-start(bf16[128,320]{0,1:T(8,128)(2,1)} %param.12) | copy-start | bytes 245764
  270.1 41.5 %all-to-all-start.6 = ((bf16[16,320,128]{2,1,0:T(8,128)(2,1)}), bf16[16,320,128]{2,1,0:T(8,128)(2,1)}, u32[]{:S(2)}, u32[]{:S(2)}) async-start(bf16[16,320,128]{2,1,0:T(8,128)(2,1)} %bitcast.129), calls=%async_computation.6 | async-start | bytes 2621440 | tf_op jit(solution)/shard_map/all_to_all | solution.py:117
Sparse Core Ops, SparseCore 0:
  15.2 42.2 all-gather.2

commit v2 on v1

--- a/solution.py
+++ b/solution.py
@@ -31,12 +31,13 @@
     hw = heads * HD
     n_ctx = lax.axis_size(CTX)
     n_chip = lax.axis_size(CHIPS)
-    n_tp = lax.axis_size(TP)
     n_z = lax.axis_size("z")
+    n_yh = lax.axis_size("yh")
+    yh = lax.axis_index("yh")
     core = lax.axis_index("core")
     chip = lax.axis_index(CHIPS)
-    tp_id = lax.axis_index(TP)
-    rows = tok // n_tp
+    z = lax.axis_index("z")
+    rows = tok // n_z
     f32, bf16 = jnp.float32, jnp.bfloat16
     scale = 1.0 / math.sqrt(HD)
     swap = [(0, 1), (1, 0)]
@@ -56,9 +57,9 @@
 
     own = latent.T
     other = lax.ppermute(own, "yh", swap)
-    is_hi = lax.axis_index("yh") == 1
-    pair = jnp.stack([jnp.where(is_hi, other, own), jnp.where(is_hi, own, other)])
+    pair = jnp.stack([jnp.where(yh == 1, other, own), jnp.where(yh == 1, own, other)])
     gathered = lax.all_gather(pair, "z", axis=0)
+    gathered, past = lax.optimization_barrier((gathered, past))
     full_t = jnp.transpose(gathered, (1, 0, 2, 3)).reshape(full, tok)
     full_rows = full_t.T
 
@@ -69,7 +70,7 @@
         out = wide * lax.rsqrt(meansq + 1e-06) * (1.0 + mod[1][None]) + mod[0][None]
         return out.astype(bf16)
 
-    own_rows = lax.dynamic_slice_in_dim(full_rows, tp_id * rows, rows, 0)
+    own_rows = lax.dynamic_slice_in_dim(full_rows, z * rows, rows, 0)
     normed = norm(full_rows, 0)
 
     chips = jnp.arange(n_chip, dtype=jnp.int32)
@@ -99,23 +100,29 @@
         out = jnp.transpose(acc / total[..., None], (1, 0, 2)).reshape(tok, hw).astype(bf16)
         return jnp.dot(out, w_out, preferred_element_type=f32).astype(bf16)
 
-    part = attend(normed).reshape(n_tp, rows, full)
-    got = lax.all_to_all(part, TP, split_axis=0, concat_axis=0, tiled=True)
-    v0_rows = jnp.sum(got.astype(f32), axis=0).astype(bf16)
+    def to_z(blocks):
+        return lax.all_to_all(blocks, "z", split_axis=0, concat_axis=0, tiled=True)
+
+    part = attend(normed).reshape(n_z, rows, full)
+    half = jnp.sum(to_z(part).astype(f32), axis=0).astype(bf16)
+    rest = lax.ppermute(half, "yh", swap)
+    v0_rows = (half.astype(f32) + rest.astype(f32)).astype(bf16)
     x1_rows = (own_rows.astype(f32) + steps[0] * v0_rows.astype(f32)).astype(bf16)
     normed_rows = norm(x1_rows, 1)
     pad = -width % 128
-    v0_send = jnp.pad(jnp.transpose(v0_rows.reshape(rows, n_tp, width), (1, 0, 2)), ((0, 0), (0, 0), (0, pad)))
-    send = jnp.concatenate([jnp.broadcast_to(normed_rows[None], (n_tp, rows, full)), v0_send], axis=2)
-    got = lax.all_to_all(send, TP, split_axis=0, concat_axis=0, tiled=True)
+    mine = lax.dynamic_index_in_dim(v0_rows.reshape(rows, n_yh, n_z, width), yh, 1, keepdims=False)
+    v0_send = jnp.pad(jnp.transpose(mine, (1, 0, 2)), ((0, 0), (0, 0), (0, pad)))
+    got = to_z(jnp.concatenate([jnp.broadcast_to(normed_rows[None], (n_z, rows, full)), v0_send], axis=2))
     normed = got[:, :, :full].reshape(tok, full)
     v0 = got[:, :, full : full + width].reshape(tok, width)
     x1 = (latent.astype(f32) + steps[0] * v0.astype(f32)).astype(bf16)
 
-    part = attend(normed)
-    part = jnp.transpose(part.reshape(tok, n_tp, width), (1, 2, 0))
-    got = lax.all_to_all(part, TP, split_axis=0, concat_axis=0, tiled=True)
-    v1 = jnp.sum(got.astype(f32), axis=0).astype(bf16).T
+    part = jnp.transpose(attend(normed).reshape(tok, n_yh, n_z, width), (2, 1, 3, 0))
+    halves = jnp.sum(to_z(part).astype(f32), axis=0).astype(bf16)
+    keep = jnp.where(yh == 1, halves[1], halves[0])
+    give = jnp.where(yh == 1, halves[0], halves[1])
+    rest = lax.ppermute(give, "yh", swap)
+    v1 = (keep.astype(f32) + rest.astype(f32)).astype(bf16).T
     x2 = (x1.astype(f32) + steps[1] * v1.astype(f32)).astype(bf16)
     return x2, jnp.stack([v0, v1])
 

time: 324 us -> 314 us (0.969)
  waiting for transfers between devices: 125 us -> 69.4 us
  blocking collectives: 57.2 us -> 111 us
  starting transfers between devices: 34.5 us -> 25.9 us
    all_to_all x1 -> x2, blocking collectives: 40.8 us -> 77.3 us  [to_z(): return lax.all_to_all(blocks, 'z', split_axis=0, concat_axis=0, tiled=True)]
    all_to_all x3 -> x1, waiting for transfers between devices: 67.7 us -> 34.5 us  [to_z(): return lax.all_to_all(blocks, 'z', split_axis=0, concat_axis=0, tiled=True)]
    all_gather x1, waiting for transfers between devices: 27.9 us -> 5.37 us  [per_device(): gathered = lax.all_gather(pair, 'z', axis=0)]
    all_to_all x1 -> x2, blocking collectives: 16.4 us -> 33.6 us  [attend(): lax.all_to_all(jnp.broadcast_to(kv[None], (n_chip, tok, 2 * hw)), CHIPS,...]
    all_to_all x3 -> x1, starting transfers between devices: 19.9 us -> 5.46 us  [to_z(): return lax.all_to_all(blocks, 'z', split_axis=0, concat_axis=0, tiled=True)]
    ppermute x0 -> x2, starting transfers between devices: none -> 5.7 us  [the longest x1 3.17 us: per_device(): rest = lax.ppermute(half, 'yh', swap)]
    unnamed x30 -> x28, local copies, waits for them, and re-layouts: 21.3 us -> 22.1 us
  transfers between devices with their start and end apart: 9 -> 9, of which waited for: 7 -> 8; matrix products, arithmetic and copies ran while one was open for 8% -> 5% of each run, Pallas kernels for 0% -> 0%
where the time goes in v2:
time: 314 us; the launch traced here: 312 us
  blocking collectives  111 us (35%)
  waiting for transfers between devices  69.4 us (22%)
  local copies, waits for them, and re-layouts  40.7 us (13%)
  starting transfers between devices  25.9 us (8%)
  matrix products  24.1 us (8%)
  other arithmetic  21.7 us (7%)
  between operations  18.9 us (6%)
    all_to_all x2, blocking collectives, to_z(): return lax.all_to_all(blocks, 'z', split_axis=0, concat_axis=0, tiled=True)  77.3 us
    all_to_all x1, waiting for transfers between devices, to_z(): return lax.all_to_all(blocks, 'z', split_axis=0, concat_axis=0, tiled=True)  34.5 us
    all_to_all x2, blocking collectives, attend(): lax.all_to_all(jnp.broadcast_to(kv[None], (n_chip, tok, 2 * hw)), CHIPS,...  33.6 us
    all_to_all x1, waiting for transfers between devices, per_device(): lax.all_to_all(hist[picked], CTX, split_axis=0, concat_axis=0, tiled=True)  23.4 us
    unnamed x28, local copies, waits for them, and re-layouts  22.1 us
    sub x2, matrix products, attend(): weights = jnp.where(live, jnp.exp(scores - top), 0.0)  9.31 us
  transfers between devices with their start and end apart: 9, of which 8 were waited for; matrix products, arithmetic and copies ran while one was open for 5% of the time, Pallas kernels for 0%

profile of v2, /device:TPU:2, one launch (start us, length us, event | category | flops | bytes accessed | tf_op | source)
XLA Modules:
  0.0 311.7 jit_solution(8635260643329205841)
XLA Ops:
  7.2 0.8 fusion.66
  8.0 1.3 gather_fusion
  9.4 0.7 copy.74
  10.1 5.9 %all-to-all-start = ((s32[16,1,1]{2,1,0:T(1,128)}), s32[16,1,1]{2,1,0:T(1,128)S(1)}, u32[]{:S(2)}, u32[]{:S(2)}) async-start(s32[16,1,1]{2,1,0:T(1,128)} %copy.74), calls=%async_computation | async-start | bytes 16384 | tf_op jit(solution)/shard_map/all_to_all | solution.py:54
  16.0 3.0 collective-permute-start
  19.0 1.1 pad_maximum_fusion.2
  20.1 0.5 all-to-all-done
  21.0 1.4 collective-permute-done
  22.4 0.9 select_bitcast_fusion.2
  23.3 0.7 pad_maximum_fusion.3
  24.0 2.0 gather_fusion.1
  26.0 5.8 %all-to-all-start.1 = ((bf16[16,128,512]{2,1,0:T(8,128)(2,1)}), bf16[16,128,512]{2,1,0:T(8,128)(2,1)}, u32[]{:S(2)}, u32[]{:S(2)}) async-start(bf16[16,128,512]{2,1,0:T(8,128)(2,1)} %gather_fusion.1), calls=%async_computation.1 | async-start | bytes 4194304 | tf_op jit(solution)/shard_map/all_to_all | solution.py:56
  31.8 0.6 fusion.76
  36.2 0.9 dynamic-slice_add_fusion
  37.1 23.4 %all-to-all-done.1 = bf16[16,128,512]{2,1,0:T(8,128)(2,1)} async-done(((bf16[16,128,512]{2,1,0:T(8,128)(2,1)}), bf16[16,128,512]{2,1,0:T(8,128)(2,1)}, u32[]{:S(2)}, u32[]{:S(2)}) %all-to-all-start.1) | async-done | bytes 2097184 | tf_op jit(solution)/shard_map/all_to_all | solution.py:56
  60.5 5.4 %all-gather.3.cloned.1.call-done = bf16[16,320,128]{2,1,0:T(8,128)(2,1)} async-done(((bf16[2,320,128]{2,1,0:T(8,128)(2,1)}), bf16[16,320,128]{2,1,0:T(8,128)(2,1)}) %all-gather.3.cloned.1.call-update) | async-done | bytes 1310736 | tf_op jit(solution)/shard_map/all_gather | solution.py:61
  65.9 1.4 copy.75
  67.3 0.8 fusion.11
  68.1 2.8 fusion.14
  71.0 0.7 convolution_convert_fusion.6
  71.7 1.5 copy-done.3
  73.2 0.7 convolution_convert_fusion.5
  74.0 16.5 %all_to_all.42 = bf16[8,128,512]{2,1,0:T(8,128)(2,1)} all-to-all(bf16[8,128,512]{2,1,0:T(8,128)(2,1)S(1)} %broadcast_in_dim.79), channel_id=1, replica_groups=mesh['yl'=2,'x'=4,'core'=2,'yh'=2,'z'=8] {'yl','x'}, dimensions={0} | all-to-all | bytes 2097152 | tf_op jit(solution)/shard_map/all_to_all | solution.py:86
  91.4 2.8 fusion.38
  94.3 2.4 pad_maximum_fusion.1
  96.7 2.3 fusion.74
  98.9 4.1 %copy.95 = bf16[4096,256]{0,1:T(8,128)(2,1)} copy(bf16[4096,256]{1,0:T(8,128)(2,1)} %get-tuple-element.16) | data formatting | bytes 4194304
  103.1 4.2 %copy.96 = bf16[4096,256]{0,1:T(8,128)(2,1)} copy(bf16[4096,256]{1,0:T(8,128)(2,1)} %get-tuple-element.17) | data formatting | bytes 4194304
  107.3 4.7 %fusion.77 = (f32[2,128]{1,0:T(2,128)S(1)}, bf16[2,128,4096]{2,1,0:T(8,128)(2,1)}) fusion(bf16[4096,2,128]{0,2,1:T(8,128)(2,1)} %bitcast.141, pred[4096]{0:T(1024)(128)(4,1)S(1)} %broadcast_bitcast_fusion, bf16[16,2,8,128]{3,2,1,0:T(8,128)(2,1)S(1)} %fusion.38), kind=kOutput, calls=%fused_computation.115 | convolution fusion | flops 274731008 | bytes 4264960 | tf_op jit(solution)/shard_map/sub | solution.py:97
  111.9 2.9 fusion.35
  114.9 1.6 convolution_convert_fusion.1
  116.5 5.5 %all-to-all-start.3 = ((bf16[8,16,5120]{2,1,0:T(8,128)(2,1)}), bf16[8,16,5120]{2,1,0:T(8,128)(2,1)}, u32[]{:S(2)}, u32[]{:S(2)}) async-start(bf16[8,16,5120]{2,1,0:T(8,128)(2,1)} %bitcast.137), calls=%async_computation.3 | async-start | bytes 2621440 | tf_op jit(solution)/shard_map/all_to_all | solution.py:104
  122.0 0.6 fusion.75
  122.6 34.5 %all-to-all-done.3 = bf16[8,16,5120]{2,1,0:T(8,128)(2,1)} async-done(((bf16[8,16,5120]{2,1,0:T(8,128)(2,1)}), bf16[8,16,5120]{2,1,0:T(8,128)(2,1)}, u32[]{:S(2)}, u32[]{:S(2)}) %all-to-all-start.3) | async-done | bytes 1310752 | tf_op jit(solution)/shard_map/all_to_all | solution.py:104
  157.1 1.5 reduce_sum.72
  158.6 3.2 %collective-permute-start.2 = (bf16[16,5120]{1,0:T(8,128)(2,1)S(1)}, bf16[16,5120]{1,0:T(8,128)(2,1)S(1)}, u32[]{:S(2)}, u32[]{:S(2)}) collective-permute-start(bf16[16,5120]{1,0:T(8,128)(2,1)S(1)} %reduce_sum.72), channel_id=1, source_target_pairs={{0,8},{8,0},{1,9},{9,1},{2,10},{10,2},{3,11},{11,3},{4,12},{12,4},... | collective-permute-start | bytes 491528 | tf_op jit(solution)/shard_map/ppermute | solution.py:108
  161.8 2.8 constant_dynamic-slice_fusion.2
  164.6 1.7 copy.94
  166.5 0.8 fusion.40
  167.5 0.7 fusion.43
  168.5 39.1 %all_to_all.43 = bf16[8,16,5504]{2,1,0:T(8,128)(2,1)S(1)} all-to-all(bf16[8,16,5504]{2,1,0:T(8,128)(2,1)S(1)} %fusion.19), channel_id=1, replica_groups=mesh['yl'=2,'x'=4,'core'=2,'yh'=2,'z'=8] {'z'}, dimensions={0} | all-to-all | bytes 2818048 | tf_op jit(solution)/shard_map/all_to_all | solution.py:104
  207.5 1.1 copy-done.8
  208.8 0.5 convolution_convert_fusion.2
  209.3 1.2 copy-done.6
  211.1 17.2 %all_to_all.44 = bf16[8,128,512]{2,1,0:T(8,128)(2,1)S(1)} all-to-all(bf16[8,128,512]{2,1,0:T(8,128)(2,1)S(1)} %broadcast_in_dim.83), channel_id=1, replica_groups=mesh['yl'=2,'x'=4,'core'=2,'yh'=2,'z'=8] {'yl','x'}, dimensions={0} | all-to-all | bytes 2097152 | tf_op jit(solution)/shard_map/all_to_all | solution.py:86
  228.3 0.5 fusion.39
  228.8 2.1 collective-permute-done.3
  231.0 1.8 pad_maximum_fusion
  232.7 2.2 fusion.73
  235.0 4.1 %copy.97 = bf16[4096,256]{0,1:T(8,128)(2,1)} copy(bf16[4096,256]{1,0:T(8,128)(2,1)} %get-tuple-element.14) | data formatting | bytes 4194304
  239.1 4.1 %copy.98 = bf16[4096,256]{0,1:T(8,128)(2,1)} copy(bf16[4096,256]{1,0:T(8,128)(2,1)} %get-tuple-element.15) | data formatting | bytes 4194304
  243.2 4.7 %fusion.80 = (f32[2,128]{1,0:T(2,128)S(1)}, bf16[2,128,4096]{2,1,0:T(8,128)(2,1)}) fusion(bf16[4096,2,128]{0,2,1:T(8,128)(2,1)} %bitcast.139, pred[4096]{0:T(1024)(128)(4,1)S(1)} %broadcast_bitcast_fusion, bf16[16,2,8,128]{3,2,1,0:T(8,128)(2,1)S(1)} %fusion.39), kind=kOutput, calls=%fused_computation.116 | convolution fusion | flops 274731008 | bytes 4264960 | tf_op jit(solution)/shard_map/sub | solution.py:97
  247.9 2.9 fusion.32
  250.8 1.6 convolution_convert_fusion
  252.4 2.4 copy.85
  254.9 1.4 copy.86
  256.3 38.2 %all_to_all.45 = bf16[8,2,320,128]{3,2,1,0:T(8,128)(2,1)} all-to-all(bf16[8,2,320,128]{3,2,1,0:T(8,128)(2,1)S(1)} %copy.86), channel_id=1, replica_groups=mesh['yl'=2,'x'=4,'core'=2,'yh'=2,'z'=8] {'z'}, dimensions={0} | all-to-all | bytes 2621440 | tf_op jit(solution)/shard_map/all_to_all | solution.py:104
  294.5 1.5 reduce_sum.75
  296.0 0.6 select_bitcast_fusion
  296.6 2.5 collective-permute-start.4
  299.2 1.5 convert_multiply_fusion.4
  300.9 1.9 collective-permute-done.4
  302.8 1.3 add_convert_fusion.1
  304.2 0.7 pad_maximum_fusion.4
  (55 shorter events, 2.7 us)
Async XLA Ops:
  7.2 107.7 %copy-start = (bf16[256,5120]{1,0:T(8,128)(2,1)S(1)}, bf16[256,5120]{1,0:T(8,128)(2,1)}, u32[]{:S(2)}) copy-start(bf16[256,5120]{1,0:T(8,128)(2,1)} %param.18) | copy-start | bytes 7864324
  10.1 10.5 %all-to-all-start = ((s32[16,1,1]{2,1,0:T(1,128)}), s32[16,1,1]{2,1,0:T(1,128)S(1)}, u32[]{:S(2)}, u32[]{:S(2)}) async-start(s32[16,1,1]{2,1,0:T(1,128)} %copy.74), calls=%async_computation | async-start | bytes 16384 | tf_op jit(solution)/shard_map/all_to_all | solution.py:54
  16.0 49.9 %all-gather.3.cloned.1.call-start = ((), (), s32[]{:S(2)}) async-start(), calls=%async_computation.7 | async-start | bytes 1474560 | tf_op jit(solution)/shard_map/all_gather | solution.py:61
  16.0 6.3 %collective-permute-start = (bf16[320,128]{1,0:T(8,128)(2,1)}, bf16[320,128]{1,0:T(8,128)(2,1)S(1)}, u32[]{:S(2)}, u32[]{:S(2)}) collective-permute-start(bf16[320,128]{1,0:T(8,128)(2,1)} %bitcast.145), channel_id=1, source_target_pairs={{0,8},{8,0},{1,9},{9,1},{2,10},{10,2},{3,11},{11,3},{4,12},{12,4},... | collective-permute-start | bytes 245768 | tf_op jit(solution)/shard_map/ppermute | solution.py:59
  26.0 5.8 %copy-start.10 = (s32[3,1]{0,1:T(1,128)S(1)}, s32[3,1]{0,1:T(1,128)}, u32[]{:S(2)}) copy-start(s32[3,1]{0,1:T(1,128)} %param.13) | copy-start | bytes 40
  26.0 34.5 %all-to-all-start.1 = ((bf16[16,128,512]{2,1,0:T(8,128)(2,1)}), bf16[16,128,512]{2,1,0:T(8,128)(2,1)}, u32[]{:S(2)}, u32[]{:S(2)}) async-start(bf16[16,128,512]{2,1,0:T(8,128)(2,1)} %gather_fusion.1), calls=%async_computation.1 | async-start | bytes 4194304 | tf_op jit(solution)/shard_map/all_to_all | solution.py:56
  67.3 4.4 %copy-start.1 = (bf16[2,8,320,128]{3,2,1,0:T(8,128)(2,1)}, bf16[2,8,320,128]{3,2,1,0:T(8,128)(2,1)S(1)}, u32[]{:S(2)}) copy-start(bf16[2,8,320,128]{3,2,1,0:T(8,128)(2,1)S(1)} %copy.75) | copy-start | bytes 3932164
  67.3 3.6 %copy-start.5 = (bf16[5120,256]{1,0:T(8,128)(2,1)S(1)}, bf16[5120,256]{1,0:T(8,128)(2,1)}, u32[]{:S(2)}) copy-start(bf16[5120,256]{1,0:T(8,128)(2,1)} %param.16) | copy-start | bytes 7864324
  71.0 2.9 copy-start.2
  71.0 2.2 copy-start.3
  90.5 3.8 %collective-permute-start.1 = (bf16[8,128,512]{2,1,0:T(8,128)(2,1)}, bf16[8,128,512]{2,1,0:T(8,128)(2,1)}, u32[]{:S(2)}, u32[]{:S(2)}) collective-permute-start(bf16[8,128,512]{2,1,0:T(8,128)(2,1)} %all_to_all.42), channel_id=1, source_target_pairs={{0,16},{16,0},{1,17},{17,1},{2,18},{18,2},{3,19},{19,3},{4,20},{20... | collective-permute-start | bytes 3145736 | tf_op jit(solution)/shard_map/ppermute | solution.py:89
  116.5 40.6 %all-to-all-start.3 = ((bf16[8,16,5120]{2,1,0:T(8,128)(2,1)}), bf16[8,16,5120]{2,1,0:T(8,128)(2,1)}, u32[]{:S(2)}, u32[]{:S(2)}) async-start(bf16[8,16,5120]{2,1,0:T(8,128)(2,1)} %bitcast.137), calls=%async_computation.3 | async-start | bytes 2621440 | tf_op jit(solution)/shard_map/all_to_all | solution.py:104
  158.6 7.9 %collective-permute-start.2 = (bf16[16,5120]{1,0:T(8,128)(2,1)S(1)}, bf16[16,5120]{1,0:T(8,128)(2,1)S(1)}, u32[]{:S(2)}, u32[]{:S(2)}) collective-permute-start(bf16[16,5120]{1,0:T(8,128)(2,1)S(1)} %reduce_sum.72), channel_id=1, source_target_pairs={{0,8},{8,0},{1,9},{9,1},{2,10},{10,2},{3,11},{11,3},{4,12},{12,4},... | collective-permute-start | bytes 491528 | tf_op jit(solution)/shard_map/ppermute | solution.py:108
  168.4 40.3 %copy-start.4 = (bf16[5120,256]{1,0:T(8,128)(2,1)S(1)}, bf16[5120,256]{1,0:T(8,128)(2,1)}, u32[]{:S(2)}) copy-start(bf16[5120,256]{1,0:T(8,128)(2,1)} %param.17) | copy-start | bytes 7864324
  207.5 1.1 copy-start.8
  208.8 1.7 copy-start.6
  211.0 17.3 %copy-start.7 = (bf16[5120,256]{1,0:T(8,128)(2,1)S(1)}, bf16[5120,256]{1,0:T(8,128)(2,1)}, u32[]{:S(2)}) copy-start(bf16[5120,256]{1,0:T(8,128)(2,1)} %param.15) | copy-start | bytes 7864324
  228.3 2.7 collective-permute-start.3
  256.3 44.4 %slice-start = ((bf16[8,16,5504]{2,1,0:T(8,128)(2,1)}), bf16[8,16,320]{2,1,0:T(8,128)(2,1)S(1)}, s32[]{:S(2)}) async-start(bf16[8,16,5504]{2,1,0:T(8,128)(2,1)} %copy-done.8), calls=%async_computation.8 | async-start | bytes 196608 | tf_op jit(solution)/shard_map/slice | solution.py:117
  256.3 46.5 %copy-start.9 = (bf16[128,320]{0,1:T(8,128)(2,1)S(1)}, bf16[128,320]{0,1:T(8,128)(2,1)}, u32[]{:S(2)}) copy-start(bf16[128,320]{0,1:T(8,128)(2,1)} %param.12) | copy-start | bytes 245764
  296.6 6.2 %collective-permute-start.4 = (bf16[320,128]{1,0:T(8,128)(2,1)}, bf16[320,128]{1,0:T(8,128)(2,1)S(1)}, u32[]{:S(2)}, u32[]{:S(2)}) collective-permute-start(bf16[320,128]{1,0:T(8,128)(2,1)} %select_bitcast_fusion), channel_id=1, source_target_pairs={{0,8},{8,0},{1,9},{9,1},{2,10},{10,2},{3,11},{11,3},{4,12},{12,4},... | collective-permute-start | bytes 245768 | tf_op jit(solution)/shard_map/ppermute | solution.py:124
Sparse Core Ops, SparseCore 0:
  24.1 41.7 all-gather.2
